TPU v7x, 32 devices: a whole 2x2x4 slice. The times are simulated.
32 devices in a mesh: dp: 8 (over z, x), tensor: 4 (over y, core).
Axes of the slice: x: 2, y: 2, z: 4, core: 2. Of those that a mesh axis runs over, the one named last changes fastest.
Arguments:
- tokens: bfloat16 [32, 1024, 1024], P('dp', 'tensor'), may hold values from -6 to 6
- cotangent: bfloat16 [32, 1024, 1024], P('dp', 'tensor'), may hold values from -6 to 6
- destination: int32 [32], replicated, may hold values from 0 to 31, as said below
- lengths: int32 [32], replicated, may hold values from 128 to 1024, as said below
- adapter_of: int32 [32], replicated, may hold values from 0 to 7
- norm_gain: bfloat16 [1024], replicated, may hold values from 0.5 to 1.5
- w_zx: bfloat16 [1024, 2, 2048], P('dp', None, 'tensor'), may hold values from -0.1875 to 0.1875
- w_bc: bfloat16 [1024, 256], P('dp'), may hold values from -0.1875 to 0.1875
- w_dt: bfloat16 [1024, 32], P('dp', 'tensor'), may hold values from -0.1875 to 0.1875
- w_out: bfloat16 [1024, 2048], P('dp', 'tensor'), may hold values from -0.125 to 0.125
- conv_x: bfloat16 [5, 2048], P(None, 'tensor'), may hold values from -3 to 3
- conv_bc: bfloat16 [5, 256], replicated, may hold values from -3 to 3
- dt_bias: float32 [32], P('tensor'), may hold values from -7 to -2.5
- a_log: float32 [32], P('tensor'), may hold values from 0 to 2.77
- d_skip: float32 [32], P('tensor'), may hold values from 0.5 to 1.5
- out_gain: bfloat16 [2048], P('tensor'), may hold values from 0.5 to 1.5
- in_down: bfloat16 [1024, 128], replicated, may hold values from -0.1875 to 0.1875
- in_up: bfloat16 [128, 2, 2048], P(None, None, 'tensor'), may hold values from -1.5 to 1.5
- out_down: bfloat16 [128, 2048], replicated, may hold values from -0.125 to 0.125
- out_up: bfloat16 [128, 1024], replicated, may hold values from -1.5 to 1.5
Outputs:
- mixed: bfloat16 [32, 1024, 1024], P('dp', 'tensor')
- token_grad: bfloat16 [32, 1024, 1024], P('dp', 'tensor')
- in_down_grad: float32 [1024, 128], replicated
- in_up_grad: float32 [128, 2, 2048], P(None, None, 'tensor')
- out_down_grad: float32 [128, 2048], replicated
- out_up_grad: float32 [128, 1024], replicated
Inputs may be any that keep to these rules, and one draw needn't show every extreme that they name: `destination`: input sequence 4 * g + p goes to slot 4 * ((g + o[p]) mod 8) + p, with one offset o[p] for each position p of a group, the same for all groups. `lengths`: of the 4 sequences dealt to the slots of one data-shard group, one has length 1024.
All inputs are finite; a program needn't handle non-finite values.
Results may differ from a plain program's by a relative error of at most 0.0095.
Values may be sent and summed in bfloat16 or wider, within the bound.
No kernel may reach another device: no remote copies, remote signals or barrier semaphores. Data moves between devices by JAX's collectives and lax.ppermute only.
A program may use at most 256 MiB of HBM per device.

v0:
```python
import jax
import jax.numpy as jnp
from jax import lax
from jax.sharding import PartitionSpec as P

INNER = 2048
HEADS = 32
NSTATE = 128
BLOCK = 256
RANK = 16


epsilon = 1e-05


def shifted(block, axis, distance):
    devices = range(lax.axis_size(axis))
    route = [((i - distance) % len(devices), i) for i in devices]
    return lax.ppermute(block, axis, route)


def einsum_high(form, *operands):
    return jnp.einsum(form, *operands, precision=lax.Precision.HIGHEST)


def rounded(values):
    return lax.optimization_barrier(values.astype(jnp.bfloat16)).astype(jnp.float32)


def silu_slope(values):
    sigmoid_part = jax.nn.sigmoid(values)
    return sigmoid_part * (1.0 + values * (1.0 - sigmoid_part))


def causal_conv(values, kernel):
    taps = kernel.shape[0] - 1
    length = values.shape[1]
    padded = jnp.pad(values, ((0, 0), (taps - 1, 0), (0, 0)))
    result = jnp.zeros_like(values) + kernel[taps]
    for offset in range(taps):
        result = result + padded[:, offset : offset + length, :] * kernel[offset]
    return result


def scan_sequence(values, steps, rate, keys_b, queries_c):
    length, heads, width = values.shape
    blocks = length // BLOCK
    value_blocks = values.reshape(blocks, BLOCK, heads, width)
    step_blocks = steps.reshape(blocks, BLOCK, heads)
    key_blocks = keys_b.reshape(blocks, BLOCK, keys_b.shape[-1])
    query_blocks = queries_c.reshape(blocks, BLOCK, queries_c.shape[-1])
    within = jnp.cumsum(step_blocks * rate, axis=1)
    lower = (jnp.arange(BLOCK)[:, None] >= jnp.arange(BLOCK)[None, :])[None, :, :, None]
    spread = within[:, :, None, :] - within[:, None, :, :]
    decay = jnp.where(lower, jnp.exp(jnp.where(lower, spread, 0.0)), 0.0)
    scores = einsum_high("ctn,csn->cts", query_blocks, key_blocks)
    weighted = value_blocks * step_blocks[..., None]
    diagonal = einsum_high("cts,ctsh,cshp->cthp", scores, decay, weighted)
    tail = jnp.exp(within[:, -1:, :] - within)
    states = einsum_high("csn,csh,cshp->chnp", key_blocks, tail, weighted)
    carry_decay = jnp.exp(within[:, -1, :])

    def advance(carry, item):
        state, factor = item
        return (factor[:, None, None] * carry + state, carry)

    start = jnp.zeros(states.shape[1:], jnp.float32)
    _, before = lax.scan(advance, start, (states, carry_decay))
    offdiag = einsum_high("ctn,chnp,cth->cthp", query_blocks, before, jnp.exp(within))
    return (diagonal + offdiag).reshape(length, heads, width)


def mix(values, steps, keys, a_log, d_skip):
    count, length, inner = values.shape
    heads = a_log.shape[0]
    split_values = values.reshape(count, length, heads, inner // heads)
    rate = -jnp.exp(a_log)

    def one_sequence(item):
        seq_values, seq_steps, seq_b, seq_c = item
        return scan_sequence(seq_values, seq_steps, rate, seq_b, seq_c)

    scanned = lax.map(
        jax.checkpoint(one_sequence), (split_values, steps, keys[..., :NSTATE], keys[..., NSTATE:])
    )
    return (scanned + d_skip[:, None] * split_values).reshape(count, length, inner)


def activate(x_part, bc_part, step_raw, conv_x, conv_bc, dt_bias):
    conv_values = jax.nn.silu(causal_conv(x_part, conv_x))
    conv_keys = jax.nn.silu(causal_conv(bc_part, conv_bc))
    steps = jax.nn.softplus(step_raw + dt_bias)
    return (conv_values, conv_keys, steps)


def on_device(
    tokens,
    cotangent,
    destination,
    lengths,
    adapter_of,
    norm_gain,
    w_zx,
    w_bc,
    w_dt,
    w_out,
    conv_x,
    conv_bc,
    dt_bias,
    a_log,
    d_skip,
    out_gain,
    in_down,
    in_up,
    out_down,
    out_up,
):
    groups = lax.axis_size("dp")
    group = lax.axis_index("dp")
    rank_index = lax.axis_index("tensor")
    seq_grp, part_len, width = tokens.shape
    places = jnp.arange(seq_grp, dtype=jnp.int32)
    offsets = destination[:seq_grp] // seq_grp
    moving = jnp.stack((tokens, cotangent))
    for level in range((groups - 1).bit_length()):
        arrived = shifted(moving, "dp", 1 << level)
        taking = offsets >> level & 1 == 1
        moving = jnp.where(taking[None, :, None, None], arrived, moving)
    sources = (group - offsets) % groups * seq_grp + places
    seq_lengths = lengths[sources]
    chosen = adapter_of[sources]
    columns = jnp.arange(in_down.shape[1], dtype=jnp.int32) // RANK
    select = (columns[None, :] == chosen[:, None]).astype(jnp.float32)
    positions = rank_index * part_len + jnp.arange(part_len, dtype=jnp.int32)
    live = (positions[None, :] < seq_lengths[:, None]).astype(jnp.float32)
    inputs = moving[0].astype(jnp.float32)
    cot_masked = moving[1].astype(jnp.float32) * live[:, :, None]
    cot_bf = cot_masked.astype(jnp.bfloat16)
    gain = norm_gain.astype(jnp.float32)
    rms = lax.rsqrt(jnp.mean(inputs * inputs, axis=-1, keepdims=True) + epsilon)
    normed_part = (inputs * rms * gain).astype(jnp.bfloat16)
    normed = lax.all_gather(normed_part, "tensor", axis=1, tiled=True)
    full_zx, full_bc, full_dt, full_out = (
        lax.all_gather(w_zx, "dp", axis=0, tiled=True),
        lax.all_gather(w_bc, "dp", axis=0, tiled=True),
        lax.all_gather(w_dt, "dp", axis=0, tiled=True),
        lax.all_gather(w_out, "dp", axis=0, tiled=True),
    )
    lowrank = (
        jnp.einsum("bld,dr->blr", normed, in_down, preferred_element_type=jnp.float32)
        * select[:, None, :]
    ).astype(jnp.bfloat16)
    both = jnp.einsum("bld,dkc->blkc", normed, full_zx, preferred_element_type=jnp.float32)
    both = both + jnp.einsum("blr,rkc->blkc", lowrank, in_up, preferred_element_type=jnp.float32)
    bc_part = jnp.einsum("bld,dn->bln", normed, full_bc, preferred_element_type=jnp.float32)
    step_raw = jnp.einsum("bld,dh->blh", normed, full_dt, preferred_element_type=jnp.float32)
    conv_float = conv_x.astype(jnp.float32)
    conv_key_float = conv_bc.astype(jnp.float32)

    def activated(x_part, bc_in, raw_steps):
        return activate(x_part, bc_in, raw_steps, conv_float, conv_key_float, dt_bias)

    (conv_values, conv_keys, steps), pull_act = jax.vjp(activated, both[:, :, 1], bc_part, step_raw)
    values_low = rounded(conv_values)
    keys_low = rounded(conv_keys)

    def mixed_local(scan_values, scan_steps, scan_keys):
        return mix(scan_values, scan_steps, scan_keys, a_log, d_skip)

    scanned, pull_mix = jax.vjp(mixed_local, values_low, steps, keys_low)
    gate_pre = both[:, :, 0]
    gated_in = scanned * jax.nn.silu(gate_pre)
    squares = lax.psum(jnp.sum(gated_in * gated_in, axis=-1), "tensor")
    scale = lax.rsqrt(squares[..., None] / INNER + epsilon)
    out_gain_float = out_gain.astype(jnp.float32)
    gated = (gated_in * scale * out_gain_float).astype(jnp.bfloat16)
    up_float = out_up.astype(jnp.float32)
    inner_part = gated.shape[2]
    down_part = lax.dynamic_slice_in_dim(out_down, rank_index * inner_part, inner_part, 1)
    side = (
        jnp.einsum("blc,rc->blr", gated, down_part, preferred_element_type=jnp.float32)
        * select[:, None, :]
    )
    terms = jnp.einsum("blc,dc->bld", gated, full_out, preferred_element_type=jnp.float32)
    terms = terms + einsum_high("blr,rd->bld", side, up_float)
    summed = lax.psum_scatter(terms, "tensor", scatter_dimension=1, tiled=True)
    cot_all = lax.all_gather(cot_bf, "tensor", axis=1, tiled=True)
    side_grad = (
        jnp.einsum("bld,rd->blr", cot_all, out_up, preferred_element_type=jnp.float32)
        * select[:, None, :]
    )
    gated_grad = jnp.einsum("bld,dc->blc", cot_all, full_out, preferred_element_type=jnp.float32)
    gated_grad = rounded(
        gated_grad + einsum_high("blr,rc->blc", side_grad, down_part.astype(jnp.float32))
    )
    up_grad_part = einsum_high("blr,bld->rd", side, cot_all.astype(jnp.float32))
    down_columns = einsum_high("blc,blr->rc", gated.astype(jnp.float32), side_grad)
    down_grad_part = lax.dynamic_update_slice_in_dim(
        jnp.zeros(out_down.shape, jnp.float32), down_columns, rank_index * inner_part, 1
    )
    mixed = (live[:, :, None] * (inputs + summed)).astype(jnp.bfloat16)
    weighted_grad = gated_grad * out_gain_float
    inner_sum = lax.psum(jnp.sum(weighted_grad * gated_in, axis=-1), "tensor")
    gated_in_grad = scale * weighted_grad - gated_in * scale**3 * inner_sum[..., None] / INNER
    scanned_grad = gated_in_grad * jax.nn.silu(gate_pre)
    gate_grad = gated_in_grad * scanned * silu_slope(gate_pre)
    values_grad, steps_grad, keys_grad = pull_mix(scanned_grad)
    xpart_grad, bc_grad, raw_grad = pull_act((values_grad, keys_grad, steps_grad))
    both_grad = jnp.stack((gate_grad, xpart_grad), axis=2).astype(jnp.bfloat16)
    up_in_part = jnp.einsum("blr,blkc->rkc", lowrank, both_grad, preferred_element_type=jnp.float32)
    down_float = in_down.astype(jnp.float32)
    heads_part = raw_grad.shape[2]
    raw_full = lax.dynamic_update_slice_in_dim(
        jnp.zeros(raw_grad.shape[:2] + (HEADS,), jnp.float32), raw_grad, rank_index * heads_part, 2
    )
    bc_rows, raw_rows = (
        lax.psum_scatter(
            bc_grad.astype(jnp.bfloat16), "tensor", scatter_dimension=1, tiled=True
        ).astype(jnp.float32),
        lax.psum_scatter(
            raw_full.astype(jnp.bfloat16), "tensor", scatter_dimension=1, tiled=True
        ).astype(jnp.float32),
    )
    grad_rows = lax.all_to_all(both_grad, "tensor", split_axis=1, concat_axis=3, tiled=True)
    dt_columns = full_dt.reshape(full_dt.shape[0], 1, heads_part)
    wide_zx, wide_up, wide_dt = (
        lax.all_gather(full_zx, "tensor", axis=2, tiled=True),
        lax.all_gather(in_up, "tensor", axis=2, tiled=True),
        lax.all_gather(dt_columns, "tensor", axis=2, tiled=True),
    )
    low_grad = (
        jnp.einsum("blkc,rkc->blr", grad_rows, wide_up, preferred_element_type=jnp.float32)
        * select[:, None, :]
    )
    normed_back = jnp.einsum(
        "blkc,dkc->bld", grad_rows, wide_zx, preferred_element_type=jnp.float32
    )
    normed_back = normed_back + einsum_high("bln,dn->bld", bc_rows, full_bc.astype(jnp.float32))
    normed_back = normed_back + einsum_high(
        "blh,dh->bld", raw_rows, wide_dt[:, 0, :].astype(jnp.float32)
    )
    normed_back = normed_back + einsum_high("blr,dr->bld", low_grad, down_float)
    down_in_part = einsum_high("bld,blr->dr", normed_part.astype(jnp.float32), low_grad)
    inner_norm = jnp.sum(gain * normed_back * inputs, axis=-1, keepdims=True)
    input_grad = cot_masked + rms * gain * normed_back - inputs * rms**3 * inner_norm / width
    in_up_grad = lax.psum(up_in_part.astype(jnp.bfloat16), "dp").astype(jnp.float32)
    in_down_grad, out_up_grad, out_down_grad = lax.psum(
        (down_in_part, up_grad_part, down_grad_part), ("dp", "tensor")
    )
    back_offsets = (groups - offsets) % groups
    returning = input_grad.astype(jnp.bfloat16)
    for level in range((groups - 1).bit_length()):
        arrived = shifted(returning, "dp", 1 << level)
        taking = back_offsets >> level & 1 == 1
        returning = jnp.where(taking[:, None, None], arrived, returning)
    return (mixed, returning, in_down_grad, in_up_grad, out_down_grad, out_up_grad)


def solution(mesh):
    return jax.shard_map(
        on_device,
        mesh=mesh,
        in_specs=(
            P("dp", "tensor", None),
            P("dp", "tensor", None),
            P(),
            P(),
            P(),
            P(),
            P("dp", None, "tensor"),
            P("dp", None),
            P("dp", "tensor"),
            P("dp", "tensor"),
            P(None, "tensor"),
            P(),
            P("tensor"),
            P("tensor"),
            P("tensor"),
            P("tensor"),
            P(),
            P(None, None, "tensor"),
            P(),
            P(),
        ),
        out_specs=(
            P("dp", "tensor", None),
            P("dp", "tensor", None),
            P(),
            P(None, None, "tensor"),
            P(),
            P(),
        ),
        check_vma=False,
    )
```

profile of v0, /device:TPU:0, one launch (start us, length us, event | category | flops | bytes accessed | tf_op | source)
XLA Modules:
  0.0 1948.4 jit_solution(11870481447195328954)
XLA Ops:
  13.6 93.0 %collective-permute-done = bf16[2,4,256,1024]{3,2,1,0:T(8,128)(2,1)S(1)} collective-permute-done((bf16[2,4,256,1024]{3,2,1,0:T(8,128)(2,1)S(1)}, bf16[2,4,256,1024]{3,2,1,0:T(8,128)(2,1)S(1)}, u32[]{:S(2)}, u32[]{:S(2)}) %collective-permute-start) | collective-permute-done | bytes 4194336 | tf_op jit(solution)/shard_map/ppermute | solution.py:19
  107.4 93.5 %collective-permute-done.1 = bf16[2,4,256,1024]{3,2,1,0:T(8,128)(2,1)S(1)} collective-permute-done((bf16[2,4,256,1024]{3,2,1,0:T(8,128)(2,1)S(1)}, bf16[2,4,256,1024]{3,2,1,0:T(8,128)(2,1)S(1)}, u32[]{:S(2)}, u32[]{:S(2)}) %collective-permute-start.1) | collective-permute-done | bytes 4194336 | tf_op jit(solution)/shard_map/ppermute | solution.py:19
  204.1 179.4 %collective-permute-done.2 = bf16[2,4,256,1024]{3,2,1,0:T(8,128)(2,1)} collective-permute-done((bf16[2,4,256,1024]{3,2,1,0:T(8,128)(2,1)}, bf16[2,4,256,1024]{3,2,1,0:T(8,128)(2,1)}, u32[]{:S(2)}, u32[]{:S(2)}) %collective-permute-start.2) | collective-permute-done | bytes 4194336 | tf_op jit(solution)/shard_map/ppermute | solution.py:19
  394.2 26.0 %all_gather.29 = bf16[1024,8]{0,1:T(8,128)(2,1)S(1)} all-gather(bf16[128,8]{0,1:T(8,128)(2,1)S(1)} %copy-done.75), channel_id=1, replica_groups=mesh['dp'=8,'tensor'=4] {'dp'}, dimensions={0}, use_global_device_ids=true | all-gather | bytes 18432 | tf_op jit(solution)/shard_map/all_gather | solution.py:146
  421.0 31.6 %all_gather.28 = bf16[1024,256]{1,0:T(8,128)(2,1)S(1)} all-gather(bf16[128,256]{1,0:T(8,128)(2,1)S(1)} %copy-done.42), channel_id=1, replica_groups=mesh['dp'=8,'tensor'=4] {'dp'}, dimensions={0}, use_global_device_ids=true | all-gather | bytes 589824 | tf_op jit(solution)/shard_map/all_gather | solution.py:145
  466.8 33.0 %all-gather.10.cloned.1.call-done = bf16[1024,2,512]{2,0,1:T(8,128)(2,1)} async-done(((bf16[128,2,512]{2,0,1:T(8,128)(2,1)}), bf16[1024,2,512]{2,0,1:T(8,128)(2,1)}) %all-gather.10.cloned.1.call-update) | async-done | bytes 2097168 | tf_op jit(solution)/shard_map/all_gather | solution.py:144
  499.8 18.8 convolution_add_fusion.2
  562.8 180.7 %while.128 = (s32[]{:T(128)}, f32[4,1024,8,64]{1,3,2,0:T(8,128)}, f32[4,1024,128]{2,1,0:T(8,128)}, f32[4,1024,128]{2,1,0:T(8,128)}, f32[4,1024,8]{1,2,0:T(8,128)...) while((s32[]{:T(128)}, f32[4,1024,8,64]{1,3,2,0:T(8,128)}, ...), condition=%wide.region_6.7_spmd.clone.clone, body=%wide.region_1.6_spmd.clone.clone.sunk | while | flops 3635625984 | bytes 60462052 | solution.py:83
  814.9 15.0 fusion.124
  846.7 507.1 %while.126 = (s32[]{:T(128)}, f32[4,1024,8,64]{1,3,2,0:T(8,128)}, f32[4,1024,8]{1,2,0:T(8,128)}, f32[4,1024,128]{2,1,0:T(8,128)}, f32[4,1024,128]{2,1,0:T(8,128)...) while((s32[]{:T(128)}, f32[4,1024,8,64]{1,3,2,0:T(8,128)}, ...), condition=%wide.region_26.27_spmd, body=%wide.region_12.26_spmd.sunk | while | flops 9303785472 | bytes 144615696 | solution.py:83
  861.4 15.1 fusion.309
  907.3 13.6 while.130
  986.9 15.1 fusion.309
  1112.7 15.1 fusion.309
  1158.6 13.5 while.130
  1238.3 15.1 fusion.309
  1284.3 13.6 while.130
  1470.3 107.1 %all-gather = bf16[1024,32]{0,1:T(8,128)(2,1)S(1)} all-gather(bf16[1024,8]{0,1:T(8,128)(2,1)S(1)} %copy-done.38), channel_id=2, replica_groups=mesh['dp'=8,'tensor'=4] {'tensor'}, dimensions={1}, use_global_device_ids=true | all-gather | bytes 81920 | tf_op jit(solution)/shard_map/all_gather | solution.py:229
  1597.4 14.9 all_to_all.16
  1622.3 17.4 fusion.121
  1647.0 49.1 %collective-permute-done.3 = bf16[4,256,1024]{2,1,0:T(8,128)(2,1)S(1)} collective-permute-done((bf16[4,256,1024]{2,1,0:T(8,128)(2,1)S(1)}, bf16[4,256,1024]{2,1,0:T(8,128)(2,1)S(1)}, u32[]{:S(2)}, u32[]{:S(2)}) %collective-permute-start.3) | collective-permute-done | bytes 2097184 | tf_op jit(solution)/shard_map/ppermute | solution.py:19
  1696.5 48.8 %collective-permute-done.4 = bf16[4,256,1024]{2,1,0:T(8,128)(2,1)S(1)} collective-permute-done((bf16[4,256,1024]{2,1,0:T(8,128)(2,1)S(1)}, bf16[4,256,1024]{2,1,0:T(8,128)(2,1)S(1)}, u32[]{:S(2)}, u32[]{:S(2)}) %collective-permute-start.4) | collective-permute-done | bytes 2097184 | tf_op jit(solution)/shard_map/ppermute | solution.py:19
  1760.8 88.6 %collective-permute-done.5 = bf16[4,256,1024]{2,1,0:T(8,128)(2,1)} collective-permute-done((bf16[4,256,1024]{2,1,0:T(8,128)(2,1)}, bf16[4,256,1024]{2,1,0:T(8,128)(2,1)}, u32[]{:S(2)}, u32[]{:S(2)}) %collective-permute-start.5) | collective-permute-done | bytes 2097184 | tf_op jit(solution)/shard_map/ppermute | solution.py:19
  1858.0 77.4 %all-reduce.21.cloned.1.call-done = (f32[1024,128]{1,0:T(8,128)}, f32[128,2048]{1,0:T(8,128)}, f32[128,1024]{1,0:T(8,128)}) async-done(((f32[1024,128]{1,0:T(8,128)}, f32[128,2048]{1,0:T(8,128)}, f32[128,1024]{1,0:T(8,128)}), (f32[1024,128]{1,0:T(8,128)}, f32[128,2048]{1,0:T(8,128)}, f32[128,1024]{1,0:T(8,128)})) %all-reduce.21.cloned.1.call-update) | async-done | bytes 2097168 | tf_op jit(solution)/shard_map/psum | solution.py:247
  (988 shorter events, 1025.7 us)
Async XLA Ops:
  7.2 784.5 %copy-start = (bf16[128,2048]{1,0:T(8,128)(2,1)S(1)}, bf16[128,2048]{1,0:T(8,128)(2,1)}, u32[]{:S(2)}) copy-start(bf16[128,2048]{1,0:T(8,128)(2,1)} %param.48) | copy-start | bytes 1572868
  7.2 445.5 %all-gather.8.cloned.1.call-start = ((), (), s32[]{:S(2)}) async-start(), calls=%async_computation.4 | async-start | bytes 10485760 | tf_op jit(solution)/shard_map/all_gather | solution.py:142
  10.0 96.6 %collective-permute-start = (bf16[2,4,256,1024]{3,2,1,0:T(8,128)(2,1)S(1)}, bf16[2,4,256,1024]{3,2,1,0:T(8,128)(2,1)S(1)}, u32[]{:S(2)}, u32[]{:S(2)}) collective-permute-start(bf16[2,4,256,1024]{3,2,1,0:T(8,128)(2,1)S(1)} %pad_maximum_fusion.1), channel_id=1, source_target_pairs={{28,0},{0,4},{4,8},{8,12},{12,16},{16,20},{20,24},{24,28},{29,1},{... | collective-permute-start | bytes 12582920 | tf_op jit(solution)/shard_map/ppermute | solution.py:19
  107.3 93.6 %collective-permute-start.1 = (bf16[2,4,256,1024]{3,2,1,0:T(8,128)(2,1)S(1)}, bf16[2,4,256,1024]{3,2,1,0:T(8,128)(2,1)S(1)}, u32[]{:S(2)}, u32[]{:S(2)}) collective-permute-start(bf16[2,4,256,1024]{3,2,1,0:T(8,128)(2,1)S(1)} %broadcast_select_fusion), channel_id=1, source_target_pairs={{24,0},{28,4},{0,8},{4,12},{8,16},{12,20},{16,24},{20,28},{25,1},{... | collective-permute-start | bytes 12582920 | tf_op jit(solution)/shard_map/ppermute | solution.py:19
  203.3 180.1 %collective-permute-start.2 = (bf16[2,4,256,1024]{3,2,1,0:T(8,128)(2,1)}, bf16[2,4,256,1024]{3,2,1,0:T(8,128)(2,1)}, u32[]{:S(2)}, u32[]{:S(2)}) collective-permute-start(bf16[2,4,256,1024]{3,2,1,0:T(8,128)(2,1)} %broadcast_select_fusion.1), channel_id=1, source_target_pairs={{16,0},{20,4},{24,8},{28,12},{0,16},{4,20},{8,24},{12,28},{17,1},{... | collective-permute-start | bytes 12582920 | tf_op jit(solution)/shard_map/ppermute | solution.py:19
  203.3 185.5 %copy-start.57 = (f32[1024]{0:T(1024)}, f32[1024]{0:T(1024)S(1)}, u32[]{:S(2)}) copy-start(f32[1024]{0:T(1024)S(1)} %convert_element_type.101) | copy-start | bytes 12292
  204.1 184.8 %copy-start.44 = (f32[4,256]{1,0:T(4,128)}, f32[4,256]{1,0:T(4,128)S(1)}, u32[]{:S(2)}) copy-start(f32[4,256]{1,0:T(4,128)S(1)} %compare_convert_fusion) | copy-start | bytes 12292
  391.4 108.4 %all-gather.10.cloned.1.call-start = ((), (), s32[]{:S(2)}) async-start(), calls=%async_computation.5 | async-start | bytes 2359296 | tf_op jit(solution)/shard_map/all_gather | solution.py:144
  392.2 382.0 %all-gather.12.cloned.1.call-start = ((), (), s32[]{:S(2)}) async-start(), calls=%async_computation.6 | async-start | bytes 1179648 | tf_op jit(solution)/shard_map/all_gather | solution.py:147
  392.9 381.2 %all-gather.14.cloned.1.call-start = ((), (), s32[]{:S(2)}) async-start(), calls=%async_computation.8 | async-start | bytes 10485760 | tf_op jit(solution)/shard_map/all_gather | solution.py:187
  420.2 135.3 %copy-start.37 = (bf16[1024,8]{0,1:T(8,128)(2,1)}, bf16[1024,8]{0,1:T(8,128)(2,1)S(1)}, u32[]{:S(2)}) copy-start(bf16[1024,8]{0,1:T(8,128)(2,1)S(1)} %all_gather.29) | copy-start | bytes 49156
  420.9 128.1 %copy-start.60 = (f32[1,256]{1,0:T(1,128)}, f32[1,256]{1,0:T(1,128)S(1)}, u32[]{:S(2)}) copy-start(f32[1,256]{1,0:T(1,128)S(1)} %get-tuple-element.940) | copy-start | bytes 3076
  452.6 1124.8 %reduce-scatter.8.cloned.1.call-start = ((), (), s32[]{:S(2)}) async-start(), calls=%async_computation.11 | async-start | bytes 327680 | tf_op jit(solution)/shard_map/reduce_scatter | solution.py:220
  846.7 509.0 %copy-start.67 = (f32[1,256]{1,0:T(1,128)S(1)}, f32[1,256]{1,0:T(1,128)}, u32[]{:S(2)}) copy-start(f32[1,256]{1,0:T(1,128)} %copy-done.66) | copy-start | bytes 3076
  1355.6 225.5 %reduce-scatter.6.cloned.1.call-start = ((), (), s32[]{:S(2)}) async-start(), calls=%async_computation.10 | async-start | bytes 2621440 | tf_op jit(solution)/shard_map/reduce_scatter | solution.py:217
  1367.4 245.0 %all-gather.18.cloned.1.call-start = ((), (), s32[]{:S(2)}) async-start(), calls=%async_computation.12 | async-start | bytes 1310720 | tf_op jit(solution)/shard_map/all_gather | solution.py:228
  1368.2 254.1 %all-gather.16.cloned.1.call-start = ((), (), s32[]{:S(2)}) async-start(), calls=%async_computation.9 | async-start | bytes 10485760 | tf_op jit(solution)/shard_map/all_gather | solution.py:227
  1369.0 389.8 %all-reduce.19.cloned.1.call-start = ((), (), s32[]{:S(2)}) async-start(), calls=%async_computation.13 | async-start | bytes 524288 | tf_op jit(solution)/shard_map/psum | solution.py:246
  1426.6 426.6 %reduce-scatter.4.cloned.1.call-start = ((), (), s32[]{:S(2)}) async-start(), calls=%async_computation.7 | async-start | bytes 20971520 | tf_op jit(solution)/shard_map/reduce_scatter | solution.py:186
  1464.5 120.5 %all-to-all-start = ((bf16[4,1024,2,512]{3,0,2,1:T(4,128)(2,1)}), bf16[4,1024,2,512]{3,0,2,1:T(4,128)(2,1)}, u32[]{:S(2)}, u32[]{:S(2)}) async-start(bf16[4,1024,2,512]{3,0,2,1:T(4,128)(2,1)} %copy.188), calls=%async_computation.1 | async-start | bytes 16777216 | tf_op jit(solution)/shard_map/all_to_all | solution.py:224
  1470.3 465.1 %all-reduce.21.cloned.1.call-start = ((), (), s32[]{:S(2)}) async-start(), calls=%async_computation.14 | async-start | bytes 4194304 | tf_op jit(solution)/shard_map/psum | solution.py:247
  1645.3 50.8 %collective-permute-start.3 = (bf16[4,256,1024]{2,1,0:T(8,128)(2,1)S(1)}, bf16[4,256,1024]{2,1,0:T(8,128)(2,1)S(1)}, u32[]{:S(2)}, u32[]{:S(2)}) collective-permute-start(bf16[4,256,1024]{2,1,0:T(8,128)(2,1)S(1)} %fusion.115), channel_id=1, source_target_pairs={{28,0},{0,4},{4,8},{8,12},{12,16},{16,20},{20,24},{24,28},{29,1},{... | collective-permute-start | bytes 6291464 | tf_op jit(solution)/shard_map/ppermute | solution.py:19
  1696.4 48.9 %collective-permute-start.4 = (bf16[4,256,1024]{2,1,0:T(8,128)(2,1)S(1)}, bf16[4,256,1024]{2,1,0:T(8,128)(2,1)S(1)}, u32[]{:S(2)}, u32[]{:S(2)}) collective-permute-start(bf16[4,256,1024]{2,1,0:T(8,128)(2,1)S(1)} %broadcast_select_fusion.3), channel_id=1, source_target_pairs={{24,0},{28,4},{0,8},{4,12},{8,16},{12,20},{16,24},{20,28},{25,1},{... | collective-permute-start | bytes 6291464 | tf_op jit(solution)/shard_map/ppermute | solution.py:19
  1746.9 102.5 %collective-permute-start.5 = (bf16[4,256,1024]{2,1,0:T(8,128)(2,1)}, bf16[4,256,1024]{2,1,0:T(8,128)(2,1)}, u32[]{:S(2)}, u32[]{:S(2)}) collective-permute-start(bf16[4,256,1024]{2,1,0:T(8,128)(2,1)} %broadcast_select_fusion.4), channel_id=1, source_target_pairs={{16,0},{20,4},{24,8},{28,12},{0,16},{4,20},{8,24},{12,28},{17,1},{... | collective-permute-start | bytes 6291464 | tf_op jit(solution)/shard_map/ppermute | solution.py:19
  (120 other events, 2586.7 us)
Sparse Core Ops, SparseCore 0:
  391.5 56.0 all-gather.7
  450.4 49.4 all-gather.9
  501.9 38.7 all-gather.11
  542.7 57.0 all-gather.13
  1355.8 19.0 reduce-scatter.7
  1377.9 31.4 reduce-scatter.5
  1411.6 16.7 all-gather.17
  1429.9 71.2 all-gather.15
  1504.6 72.5 all-reduce.18
  1579.7 125.3 reduce-scatter.3
  1758.9 176.4 all-reduce.20
where the time goes:
time: 1960 us; the launch traced here: 1950 us
  waiting for transfers between devices  664 us (34%)
  matrix products  465 us (24%)
  local copies, waits for them, and re-layouts  328 us (17%)
  other arithmetic  266 us (14%)
  blocking collectives  175 us (9%)
  loops' own time  23.5 us (1%)
    ppermute x6, waiting for transfers between devices, shifted(): return lax.ppermute(block, axis, route)  552 us
    dot_general x64, matrix products, einsum_high(): return jnp.einsum(form, *operands, precision=lax.Precision.HIGHEST)  358 us
    all_gather x1, blocking collectives, on_device(): lax.all_gather(dt_columns, 'tensor', axis=2, tiled=True)  107 us
    psum x1, waiting for transfers between devices, on_device(): lax.psum((down_in_part, up_grad_part, down_grad_part), ('dp', 'tensor'))  77.4 us
    another operation x45, other arithmetic  63.6 us
    dynamic_slice x96, local copies, waits for them, and re-layouts, scan_sequence(): _, before = lax.scan(advance, start, (states, carry_decay))  40.9 us
  transfers between devices with their start and end apart: 18, of which 8 were waited for; matrix products, arithmetic and copies ran while one was open for 24% of the time, Pallas kernels for 0%

commit v1 on v0

v1 whole, which is shorter than its diff:
```python
import functools

import jax
import jax.numpy as jnp
from jax import lax
from jax.experimental import pallas as pl
from jax.experimental.pallas import tpu as pltpu
from jax.sharding import PartitionSpec as P

RANK = 16
SCAN = 128
ROWS = 256
TILE = 256
HEAD = 64
EPS = 1e-05
LIMIT = 56 * 1024 * 1024

f32 = jnp.float32
bf16 = jnp.bfloat16
ANY = pl.BlockSpec(memory_space=pl.ANY)
SMEM = pl.BlockSpec(memory_space=pltpu.SMEM)


def nn(a, b):
    return lax.dot_general(a, b, (((1,), (0,)), ((), ())), preferred_element_type=f32)


def nt(a, b):
    return lax.dot_general(a, b, (((1,), (1,)), ((), ())), preferred_element_type=f32)


def tn(a, b):
    return lax.dot_general(a, b, (((0,), (0,)), ((), ())), preferred_element_type=f32)


def exact(a, b):
    return lax.dot_general(
        a, b, (((1,), (0,)), ((), ())), preferred_element_type=f32, precision=lax.Precision.HIGHEST
    )


def halves(v, axis):
    high = v.astype(bf16)
    low = (v - high.astype(f32)).astype(bf16)
    return jnp.concatenate([high, low], axis=axis)


def sigmoid(v):
    return 1.0 / (1.0 + jnp.exp(-v))


def softplus(v):
    return jnp.maximum(v, 0.0) + jnp.log1p(jnp.exp(-jnp.abs(v)))


def triangle(n, lower):
    row = lax.broadcasted_iota(jnp.int32, (n, n), 0)
    col = lax.broadcasted_iota(jnp.int32, (n, n), 1)
    return row >= col if lower else row <= col


def head_vectors(vec, parts):
    width = vec.shape[1] // parts
    total = vec[8:16, 0:128]
    for t in range(1, parts):
        total = total + vec[8:16, t * width : t * width + 128]
    return total


def split_lanes(v):
    low_lanes = lax.broadcasted_iota(jnp.int32, v.shape, 1) < HEAD
    return jnp.where(low_lanes, v, 0.0).astype(bf16), jnp.where(low_lanes, 0.0, v).astype(bf16)


class Pieces:
    def __init__(self, arrays, moves):
        self.arrays, self.moves = arrays, moves


def copy_in(info, groups, sems):
    copies = []
    for refs, moves, full in groups:
        for which, index, take, place in moves:
            src = refs[which]
            if index is not None:
                src = src.at[index]
            if take is not None:
                src = src.at[take]
            copies.append(pltpu.make_async_copy(src, place(info, full), sems.at[len(copies)]))
    for copy in copies:
        copy.start()
    for copy in copies:
        copy.wait()


def whole_block(shape):
    return pl.BlockSpec(shape, lambda c: (0,) * len(shape))


def row_block(width, rows=ROWS):
    return pl.BlockSpec((rows, width), lambda c: (c, 0))


def take_refs(refs, counts):
    taken, at = [], 0
    for count in counts:
        taken.append(refs[at : at + count])
        at += count
    return taken, refs[at:]


def scan_kernel(names, moves, counts, parts, heads, *refs):
    info, gain, in_down, convbc, spread_heads = refs[:5]
    groups, rest = take_refs(refs[5:], counts)
    (x_out, w_full, bc_full, dt_full, vec, up, normed_out, low_out, pre_out, values_out, scanned_out) = rest[:11]
    (keys_out, prebc_out, scal_out, states_out, xs, dt_wide, xbuf, bcbuf, state, sems) = rest[11:]
    fulls = dict(x=xs, w=w_full, bc=bc_full, dt=dt_wide, up=up, vec=vec)
    c = pl.program_id(0)
    inner = w_full.shape[1]
    subs = ROWS // SCAN

    @pl.when(c == 0)
    def _():
        copy_in(info, [(groups[g], m, fulls[name]) for name, g, m in zip(names, moves[0], moves[1])], sems)
        state[...] = jnp.zeros_like(state)
        xbuf[0:8, :] = jnp.zeros((8, inner), f32)
        bcbuf[0:8, :] = jnp.zeros((8, bcbuf.shape[1]), f32)
        own = heads // parts
        dt_full[...] = jnp.concatenate(
            [dt_wide[16 * t : 16 * t + 16, :].astype(f32)[:own] for t in range(parts)], axis=0
        ).astype(bf16)

    x_low = xs[pl.ds(pl.multiple_of(c * ROWS, ROWS), ROWS), :]
    x_out[...] = x_low
    x = x_low.astype(f32)
    rms = lax.rsqrt(jnp.mean(x * x, axis=1, keepdims=True) + EPS)
    normed_out[...] = (x * rms * gain[...]).astype(bf16)
    low_out[...] = nn(normed_out[...], in_down[...]).astype(bf16)
    hv = head_vectors(vec, parts)
    bias, rate = hv[0:1, 0:heads], -jnp.exp(hv[1:2, 0:heads])

    bcbuf[8:, :] = nn(normed_out[...], bc_full[...])
    pre = convbc[4:5, :] + sum(convbc[k : k + 1, :] * bcbuf[5 + k : 5 + k + ROWS, :] for k in range(4))
    bcbuf[0:8, :] = bcbuf[ROWS : ROWS + 8, :]
    prebc_out[...] = pre
    keys_out[...] = (pre * sigmoid(pre)).astype(bf16)
    nstate = keys_out.shape[1] // 2

    raw = nt(normed_out[...], dt_full[...]) + bias
    steps = softplus(raw)
    lower = triangle(SCAN, True)
    lower_f = lower.astype(f32)
    cums, cum_rows, grown, scores, key_cols = [], [], [], [], []
    for s in range(subs):
        rows = slice(s * SCAN, (s + 1) * SCAN)
        dt_s = steps[rows]
        cum = exact(lower_f, dt_s * rate)
        cums.append(cum)
        cum_rows.append(cum.T)
        b_part, c_part = keys_out[rows, 0:nstate], keys_out[rows, nstate:]
        scores.append(jnp.where(lower, nt(c_part, b_part), 0.0))
        key_cols.append(b_part.astype(f32).T.astype(bf16))
        tail = jnp.exp(cum[SCAN - 1 : SCAN, :] - cum)
        grown.append((halves(dt_s, 1), halves(jnp.exp(cum), 1), halves(dt_s * tail, 1)))
    scal_out[...] = jnp.concatenate(
        [steps, jnp.concatenate(cums, axis=0), sigmoid(raw), jnp.zeros((ROWS, 128 - 3 * heads), f32)], axis=1
    )

    for j in range(inner // TILE):
        cols = slice(j * TILE, (j + 1) * TILE)
        xbuf[8:, cols] = nn(normed_out[...], w_full[:, cols]) + nn(low_out[...], up[:, cols])
        pre = vec[4:5, cols] + sum(vec[k : k + 1, cols] * xbuf[5 + k : 5 + k + ROWS, cols] for k in range(4))
        xbuf[0:8, cols] = xbuf[ROWS : ROWS + 8, cols]
        pre_out[:, cols] = pre.astype(bf16)
        values_out[:, cols] = (pre * sigmoid(pre)).astype(bf16)
        for s in range(subs):
            rows = slice(s * SCAN, (s + 1) * SCAN)
            dtx, ecx, tlx = (nn(v, spread_heads[:, cols]) for v in grown[s])
            state_low = state[:, cols].astype(bf16)
            states_out[s, :, cols] = state_low
            v = values_out[rows, cols].astype(f32)
            y = ecx * nn(keys_out[rows, nstate:], state_low) + vec[6:7, cols] * v
            vw = v * dtx
            within = []
            for p in range(TILE // 128):
                lhs = []
                for a in range(2):
                    h = (j * TILE + p * 128) // HEAD + a
                    gap = cums[s][:, h : h + 1] - cum_rows[s][h : h + 1, :]
                    lhs.append((jnp.exp(jnp.minimum(gap, 0.0)) * scores[s]).astype(bf16))
                rhs = jnp.concatenate(split_lanes(vw[:, p * 128 : (p + 1) * 128]), axis=0)
                within.append(nn(jnp.concatenate(lhs, axis=1), rhs))
            scanned_out[rows, cols] = y + jnp.concatenate(within, axis=1)
            state[:, cols] = ecx[SCAN - 1 : SCAN, :] * state[:, cols] + nn(key_cols[s], (v * tlx).astype(bf16))


def call_scan(info, gain, in_down, convbc, spread_heads, pieces, parts, heads, length, width, inner):
    names = ("x", "w", "bc", "dt", "up", "vec")
    owners, lists, arrays, counts = [], [], [], []
    for i, name in enumerate(names):
        owners.append(i)
        lists.append(pieces[name].moves)
        arrays += pieces[name].arrays
        counts.append(len(pieces[name].arrays))
    total = sum(len(m) for m in lists)
    two_n = convbc.shape[1]
    steps, subs = length // ROWS, ROWS // SCAN
    shapes = [
        ((length, width), bf16), ((width, inner), bf16), ((width, two_n), bf16), ((heads, width), bf16),
        ((16, inner), f32), ((RANK, inner), bf16), ((length, width), bf16), ((length, RANK), bf16),
        ((length, inner), bf16), ((length, inner), bf16), ((length, inner), f32), ((length, two_n), bf16),
        ((length, two_n), f32), ((length, 128), f32), ((length // SCAN, two_n // 2, inner), bf16),
    ]
    specs = [
        row_block(width), whole_block((width, inner)), whole_block((width, two_n)), whole_block((heads, width)),
        whole_block((16, inner)), whole_block((RANK, inner)), row_block(width), row_block(RANK),
        row_block(inner), row_block(inner), row_block(inner), row_block(two_n),
        row_block(two_n), row_block(128), pl.BlockSpec((subs, two_n // 2, inner), lambda c: (c, 0, 0)),
    ]
    return pl.pallas_call(
        functools.partial(scan_kernel, names, (owners, lists), counts, parts, heads),
        grid=(steps,),
        in_specs=[SMEM, whole_block(gain.shape), whole_block(in_down.shape), whole_block(convbc.shape)]
        + [whole_block(spread_heads.shape)] + [ANY] * len(arrays),
        out_shape=[jax.ShapeDtypeStruct(s, d) for s, d in shapes],
        out_specs=specs,
        scratch_shapes=[
            pltpu.VMEM((length, width), bf16), pltpu.VMEM((parts * 16, width), bf16),
            pltpu.VMEM((ROWS + 8, inner), f32), pltpu.VMEM((ROWS + 8, two_n), f32),
            pltpu.VMEM((two_n // 2, inner), f32), pltpu.SemaphoreType.DMA((total,)),
        ],
        compiler_params=pltpu.CompilerParams(vmem_limit_bytes=LIMIT, dimension_semantics=("arbitrary",)),
    )(info, gain, in_down, convbc, spread_heads, *arrays)


def gate_kernel(names, moves, counts, *refs):
    info, normed, low, scanned, x, vec, head_sum, out_down, out_up = refs[:9]
    groups, rest = take_refs(refs[9:], counts)
    (mixed_out, dlayer_out, dy_out, dot_out, back_out, low_back_out, in_up_out, out_down_out, out_up_out) = rest[:9]
    (wz, wo, upz, cots, z, gi, gated, gg, zg, sems) = rest[9:]
    fulls = dict(z=wz, o=wo, up=upz, cot=cots)
    c = pl.program_id(0)
    inner = wz.shape[1]
    tiles = [slice(j * TILE, (j + 1) * TILE) for j in range(inner // TILE)]

    @pl.when(c == 0)
    def _():
        copy_in(info, [(groups[g], m, fulls[name]) for name, g, m in zip(names, moves[0], moves[1])], sems)
        in_up_out[...] = jnp.zeros_like(in_up_out)
        out_down_out[...] = jnp.zeros_like(out_down_out)
        out_up_out[...] = jnp.zeros_like(out_up_out)

    squares = jnp.zeros((ROWS, TILE), f32)
    for cols in tiles:
        zj = nn(normed[...], wz[:, cols]) + nn(low[...], upz[:, cols])
        z[:, cols] = zj
        g = scanned[:, cols] * (zj * sigmoid(zj))
        gi[:, cols] = g
        squares = squares + g * g
    scale = lax.rsqrt(jnp.sum(squares, axis=1, keepdims=True) / inner + EPS)
    for cols in tiles:
        gated[:, cols] = (gi[:, cols] * scale * vec[5:6, cols]).astype(bf16)
    side = nt(gated[...], out_down[...]).astype(bf16)
    terms = nt(gated[...], wo[...]) + nn(side, out_up[...])
    rows = lax.broadcasted_iota(jnp.int32, (ROWS, 1), 0) + c * ROWS
    live = rows < info[0]
    mixed_out[...] = jnp.where(live, x[...].astype(f32) + terms, 0.0).astype(bf16)
    cot = cots[pl.ds(pl.multiple_of(c * ROWS, ROWS), ROWS), :]
    dlayer_out[...] = jnp.where(live, cot.astype(f32), 0.0).astype(bf16)
    side_grad = nt(dlayer_out[...], out_up[...]).astype(bf16)
    inner_dot = jnp.zeros((ROWS, TILE), f32)
    for cols in tiles:
        grad = (nn(dlayer_out[...], wo[:, cols]) + nn(side_grad, out_down[:, cols])).astype(bf16)
        gg[:, cols] = grad
        inner_dot = inner_dot + grad.astype(f32) * vec[5:6, cols] * gi[:, cols]
    factor = scale * scale * scale * (jnp.sum(inner_dot, axis=1, keepdims=True) / inner)
    dots = jnp.zeros((ROWS, head_sum.shape[1]), f32)
    for cols in tiles:
        grad = scale * (gg[:, cols].astype(f32) * vec[5:6, cols]) - gi[:, cols] * factor
        zj = z[:, cols]
        sig = sigmoid(zj)
        sc = scanned[:, cols]
        dy = (grad * (zj * sig)).astype(bf16)
        dy_out[:, cols] = dy
        zg[:, cols] = (grad * sc * (sig * (1.0 + zj * (1.0 - sig)))).astype(bf16)
        summer = head_sum[cols, :]
        dots = dots + nn(halves(dy.astype(f32) * sc, 1), jnp.concatenate([summer, summer], axis=0))
    dot_out[...] = dots
    back_out[...] = nt(zg[...], wz[...])
    low_back_out[...] = nt(zg[...], upz[...])
    in_up_out[...] += tn(low[...], zg[...])
    out_down_out[...] += tn(side_grad, gated[...])
    out_up_out[...] += tn(side, dlayer_out[...])


def call_gate(info, normed, low, scanned, x, vec, head_sum, out_down, out_up, pieces):
    names = ("z", "o", "up", "cot")
    owners, lists, arrays, counts = [], [], [], []
    for i, name in enumerate(names):
        owners.append(i)
        lists.append(pieces[name].moves)
        arrays += pieces[name].arrays
        counts.append(len(pieces[name].arrays))
    total = sum(len(m) for m in lists)
    length, width = x.shape
    inner, heads = head_sum.shape
    shapes = [
        ((length, width), bf16), ((length, width), bf16), ((length, inner), bf16), ((length, heads), f32),
        ((length, width), f32), ((length, RANK), f32), ((RANK, inner), f32), ((RANK, inner), f32),
        ((RANK, width), f32),
    ]
    specs = [
        row_block(width), row_block(width), row_block(inner), row_block(heads), row_block(width), row_block(RANK),
        whole_block((RANK, inner)), whole_block((RANK, inner)), whole_block((RANK, width)),
    ]
    return pl.pallas_call(
        functools.partial(gate_kernel, names, (owners, lists), counts),
        grid=(length // ROWS,),
        in_specs=[SMEM, row_block(width), row_block(RANK), row_block(inner), row_block(width), whole_block(vec.shape)]
        + [whole_block(head_sum.shape), whole_block(out_down.shape), whole_block(out_up.shape)] + [ANY] * len(arrays),
        out_shape=[jax.ShapeDtypeStruct(s, d) for s, d in shapes],
        out_specs=specs,
        scratch_shapes=[
            pltpu.VMEM((width, inner), bf16), pltpu.VMEM((width, inner), bf16), pltpu.VMEM((RANK, inner), bf16),
            pltpu.VMEM((length, width), bf16), pltpu.VMEM((ROWS, inner), f32), pltpu.VMEM((ROWS, inner), f32),
            pltpu.VMEM((ROWS, inner), bf16), pltpu.VMEM((ROWS, inner), bf16), pltpu.VMEM((ROWS, inner), bf16),
            pltpu.SemaphoreType.DMA((total,)),
        ],
        compiler_params=pltpu.CompilerParams(vmem_limit_bytes=LIMIT, dimension_semantics=("arbitrary",)),
    )(info, normed, low, scanned, x, vec, head_sum, out_down, out_up, *arrays)


def back_kernel(parts, heads, *refs):
    (x, normed, low, dlayer, dy, values, pre, keys, prebc, scal, states, dot, back, low_back) = refs[:14]
    (w_full, bc_full, dt_full, vec, up, gain, in_down, convbc, spread_heads, head_sum) = refs[14:24]
    (grad_out, in_up_out, in_down_out, dstate, xbuf, bcbuf, xg, summed) = refs[24:]
    i = pl.program_id(0)
    inner = w_full.shape[1]
    subs = ROWS // SCAN
    nstate = keys.shape[1] // 2
    tiles = [slice(j * TILE, (j + 1) * TILE) for j in range(inner // TILE)]

    @pl.when(i == 0)
    def _():
        dstate[...] = jnp.zeros_like(dstate)
        xbuf[ROWS:, :] = jnp.zeros((8, inner), f32)
        bcbuf[ROWS:, :] = jnp.zeros((8, bcbuf.shape[1]), f32)
        summed[...] = jnp.zeros_like(summed)
        in_up_out[...] = jnp.zeros_like(in_up_out)
        in_down_out[...] = jnp.zeros_like(in_down_out)

    hv = head_vectors(vec, parts)
    rate = -jnp.exp(hv[1:2, 0:heads])
    upper = triangle(SCAN, False)
    upper_f = upper.astype(f32)
    raw_parts = [None] * subs
    for s in reversed(range(subs)):
        rows = slice(s * SCAN, (s + 1) * SCAN)
        steps, cum = scal[rows, 0:heads], scal[rows, heads : 2 * heads]
        cum_row = cum.T
        last = cum[SCAN - 1 : SCAN, :]
        dt2, ecum2, tail2 = halves(steps, 1), halves(jnp.exp(cum), 1), halves(jnp.exp(last - cum), 1)
        b_part, c_part = keys[rows, 0:nstate], keys[rows, nstate:]
        c_cols = c_part.astype(f32).T.astype(bf16)
        scores = jnp.where(upper, nt(b_part, c_part), 0.0)
        pulled = jnp.zeros((SCAN, SCAN), f32)
        c_grad = jnp.zeros((SCAN, nstate), f32)
        b_grad = jnp.zeros((SCAN, nstate), f32)
        direct = jnp.zeros((SCAN, heads), f32)
        through = jnp.zeros((SCAN, heads), f32)
        for j, cols in enumerate(tiles):
            dtx, ecx, tlx = (nn(v, spread_heads[:, cols]) for v in (dt2, ecum2, tail2))
            g_low = dy[rows, cols]
            g = g_low.astype(f32)
            v = values[rows, cols].astype(f32)
            vw = v * dtx
            dstate_low = dstate[:, cols].astype(bf16)
            within = []
            for p in range(TILE // 128):
                part = slice(p * 128, (p + 1) * 128)
                vw_split = split_lanes(vw[:, part])
                lhs = []
                for a in range(2):
                    h = (j * TILE + p * 128) // HEAD + a
                    gap = cum_row[h : h + 1, :] - cum[:, h : h + 1]
                    decay = jnp.exp(jnp.minimum(gap, 0.0))
                    pulled = pulled + decay * nt(vw_split[a], g_low[:, part])
                    lhs.append((decay * scores).astype(bf16))
                rhs = jnp.concatenate(split_lanes(g[:, part]), axis=0)
                within.append(nn(jnp.concatenate(lhs, axis=1), rhs))
            dvw = jnp.concatenate(within, axis=1) + tlx * nn(b_part, dstate_low)
            vg = dtx * dvw + vec[6:7, cols] * g
            summer = head_sum[cols, :]
            summer = jnp.concatenate([summer, summer], axis=0)
            direct = direct + nn(halves(v * dvw, 1), summer)
            through = through + nn(halves(v * vg, 1), summer)
            ge = (ecx * g).astype(bf16)
            c_grad = c_grad + nt(ge, states[s, :, cols])
            b_grad = b_grad + nt((tlx * vw).astype(bf16), dstate_low)
            dstate[:, cols] = ecx[SCAN - 1 : SCAN, :] * dstate[:, cols] + nn(c_cols, ge)
            pv = pre[rows, cols].astype(f32)
            sig = sigmoid(pv)
            xbuf[rows, cols] = vg * (sig * (1.0 + pv * (1.0 - sig)))
        pulled = jnp.where(upper, pulled, 0.0)
        b_grad = b_grad + nn(pulled.astype(bf16), c_part)
        c_grad = c_grad + nn(pulled.T.astype(bf16), b_part)
        pb = prebc[rows, :]
        sig = sigmoid(pb)
        bcbuf[rows, :] = jnp.concatenate([b_grad, c_grad], axis=1) * (sig * (1.0 + pb * (1.0 - sig)))
        change = dot[rows, :] - through
        later = exact(upper_f, change) + summed[0:1, 0:heads]
        summed[0:1, 0:heads] = later[0:1, :]
        raw_parts[s] = (direct + rate * later) * scal[rows, 2 * heads : 3 * heads]
    raw_grad = jnp.concatenate(raw_parts, axis=0).astype(bf16)

    for cols in tiles:
        xg[:, cols] = sum(vec[k : k + 1, cols] * xbuf[3 - k : 3 - k + ROWS, cols] for k in range(4)).astype(bf16)
    xbuf[ROWS:, :] = xbuf[0:8, :]
    bc_grad = sum(convbc[k : k + 1, :] * bcbuf[3 - k : 3 - k + ROWS, :] for k in range(4)).astype(bf16)
    bcbuf[ROWS:, :] = bcbuf[0:8, :]
    low_grad = (low_back[...] + nt(xg[...], up[...])).astype(bf16)
    in_up_out[...] += tn(low[...], xg[...])
    in_down_out[...] += tn(low_grad, normed[...])
    ng = back[...] + nt(xg[...], w_full[...]) + nt(bc_grad, bc_full[...])
    ng = ng + nn(raw_grad, dt_full[...]) + nt(low_grad, in_down[...])
    xv = x[...].astype(f32)
    rms = lax.rsqrt(jnp.mean(xv * xv, axis=1, keepdims=True) + EPS)
    ng = ng * gain[...]
    inner_norm = jnp.mean(ng * xv, axis=1, keepdims=True)
    grad_out[...] = (dlayer[...].astype(f32) + rms * ng - xv * (rms * rms * rms * inner_norm)).astype(bf16)


def call_back(rows_in, consts, parts, heads):
    x, w_full = rows_in[0], consts[0]
    length, width = x.shape
    inner = w_full.shape[1]
    two_n = rows_in[7].shape[1]
    steps, subs = length // ROWS, ROWS // SCAN

    def spec(a):
        if a.ndim == 3:
            return pl.BlockSpec((subs,) + a.shape[1:], lambda i: (steps - 1 - i, 0, 0))
        return pl.BlockSpec((ROWS, a.shape[1]), lambda i: (steps - 1 - i, 0))

    return pl.pallas_call(
        functools.partial(back_kernel, parts, heads),
        grid=(steps,),
        in_specs=[spec(a) for a in rows_in] + [whole_block(a.shape) for a in consts],
        out_shape=[
            jax.ShapeDtypeStruct((length, width), bf16),
            jax.ShapeDtypeStruct((RANK, inner), f32),
            jax.ShapeDtypeStruct((RANK, width), f32),
        ],
        out_specs=[spec(x), whole_block((RANK, inner)), whole_block((RANK, width))],
        scratch_shapes=[
            pltpu.VMEM((two_n // 2, inner), f32), pltpu.VMEM((ROWS + 8, inner), f32),
            pltpu.VMEM((ROWS + 8, two_n), f32), pltpu.VMEM((ROWS, inner), bf16), pltpu.VMEM((8, 128), f32),
        ],
        compiler_params=pltpu.CompilerParams(vmem_limit_bytes=LIMIT, dimension_semantics=("arbitrary",)),
    )(*rows_in, *consts)


def moved(block, axis, route):
    size = lax.axis_size(axis)
    return lax.ppermute(block, axis, [(i, route(i, size)) for i in range(size)])


def near(axis):
    return [lambda block: moved(block, axis, lambda i, n: i ^ 1)]


def far(axis):
    return [
        functools.partial(lambda k, block: moved(block, axis, lambda i, n: (i + 2 * k) % n), k)
        for k in range(1, lax.axis_size(axis) // 2)
    ]


def spread(block, order):
    stages = dict(z=far("dp"), x=near("dp"), y=far("tensor"), c=near("tensor"))
    held, labels = block[None], [dict(z=0, x=0, y=0, c=0)]
    for at, name in enumerate(order):
        got = [move(held) for move in stages[name]]
        lists = [labels] + [[dict(label, **{name: k + 1}) for label in labels] for k in range(len(got))]
        if at == len(order) - 1:
            return [held] + got, lists
        held = jnp.concatenate([held] + got, axis=0)
        labels = sum(lists, [])
    return None


def index_table(length_of, groups, parts, group, rank):
    dp_from = [((group ^ kx) - 2 * kz) % groups for kz in range(groups // 2) for kx in range(2)]
    part_from = [((rank ^ kc) - 2 * ky) % parts for ky in range(parts // 2) for kc in range(2)]
    partner = [rank ^ k for k in range(parts)]
    return jnp.stack([length_of] + dp_from + part_from + partner).astype(jnp.int32)


def placed(gathered, groups, take, place):
    arrays, lists = gathered
    moves = []
    for which, labels in enumerate(lists):
        for index, label in enumerate(labels):
            g_at = 1 + label["z"] * 2 + label["x"]
            t_at = 1 + groups + label["y"] * 2 + label["c"]
            moves.append((which, index, take, functools.partial(
                lambda g_at, t_at, info, full: place(info[g_at], info[t_at], full), g_at, t_at)))
    return Pieces(list(arrays), moves)


def paired(arrays, groups, parts, index, place):
    moves = [
        (k, index, None, functools.partial(lambda at, info, full: place(info[at], full), 1 + groups + parts + k))
        for k in range(parts)
    ]
    return Pieces(list(arrays), moves)


def single(array):
    return Pieces([array], [(0, None, None, lambda info, full: full)])


def span(index, size):
    return pl.ds(pl.multiple_of(index * size, size), size)


def exchanged(blocks):
    return [
        block if k == 0 else moved(block, "tensor", functools.partial(lambda k, i, n: i ^ k, k))
        for k, block in enumerate(blocks)
    ]


def dealt(block, offset, group):
    groups = lax.axis_size("dp")
    odd = offset % 2 == 1
    block = jnp.where(odd, moved(block, "dp", lambda i, n: i ^ 1), block)
    hops = offset // 2 + jnp.where(odd & (group % 2 == 0), 1, 0)
    for level in range((groups // 2 - 1).bit_length()):
        arrived = moved(block, "dp", functools.partial(lambda step, i, n: (i + step) % n, 2 << level))
        block = jnp.where(hops >> level & 1 == 1, arrived, block)
    return block


def on_device(
    tokens, cotangent, destination, lengths, adapter_of, norm_gain, w_zx, w_bc, w_dt, w_out,
    conv_x, conv_bc, dt_bias, a_log, d_skip, out_gain, in_down, in_up, out_down, out_up,
):
    groups, parts = lax.axis_size("dp"), lax.axis_size("tensor")
    group, rank = lax.axis_index("dp"), lax.axis_index("tensor")
    seq_grp, part_len, width = tokens.shape
    rows, _, cols = w_zx.shape
    own_heads = w_dt.shape[1]
    length, inner, heads = part_len * parts, cols * parts, own_heads * parts
    places = jnp.arange(seq_grp, dtype=jnp.int32)
    offsets = destination[:seq_grp] // seq_grp
    mine = group * seq_grp + rank
    adapter = adapter_of[mine] * RANK
    info = index_table(lengths[mine], groups, parts, group, rank)

    def rows_of(array):
        return exchanged([lax.dynamic_index_in_dim(array, rank ^ k, 0, keepdims=False) for k in range(parts)])

    def row_place(t, full):
        return full.at[span(t, part_len), :]

    x_pieces = paired(rows_of(tokens), groups, parts, None, row_place)

    own_vec = jnp.concatenate(
        [conv_x.astype(f32), out_gain.astype(f32)[None], jnp.repeat(d_skip, cols // own_heads)[None], jnp.zeros((1, cols), f32)]
    )
    own_heads_vec = lax.dynamic_update_slice(
        jnp.zeros((8, cols), f32), jnp.stack([dt_bias, a_log]), (0, rank * own_heads)
    )
    own_vec = jnp.concatenate([own_vec, own_heads_vec])

    def col_place(t, full):
        return full.at[:, span(t, cols)]

    vec_pieces = paired(exchanged([own_vec] * parts), groups, parts, None, col_place)
    ups = []
    for k in range(parts):
        theirs = adapter_of[group * seq_grp + (rank ^ k)] * RANK
        ups.append(lax.dynamic_slice_in_dim(in_up, theirs, RANK, 0).transpose(1, 0, 2))
    ups = exchanged(ups)
    up_x, up_z = (paired(ups, groups, parts, k, col_place) for k in (1, 0))

    order = ("z", "x", "y", "c")

    def block_place(g, t, full):
        return full.at[span(g, rows), span(t, cols)]

    x_weights = placed(spread(w_zx[:, 1], order), groups, None, block_place)
    share = rows // parts
    if share % 16 == 0 and rows % 128 == 0:
        own_bc = lax.dynamic_slice_in_dim(w_bc, rank * share, share, 0)
        own_dt = jnp.zeros((16, w_bc.shape[1]), bf16).at[:own_heads, :rows].set(w_dt.T)
        small = spread(jnp.concatenate([own_bc, own_dt]), order)
        bc_weights = placed(
            small, groups, (pl.ds(0, share),), lambda g, t, full: full.at[span(g * parts + t, share), :]
        )
        dt_weights = placed(
            small, groups, (pl.ds(share, 16), pl.ds(0, rows)), lambda g, t, full: full.at[span(t, 16), span(g, rows)]
        )
        dt_weights.arrays = bc_weights.arrays
    else:
        bc_weights = single(lax.all_gather(w_bc, "dp", axis=0, tiled=True))
        all_dt = lax.all_gather(lax.all_gather(w_dt, "dp", axis=0, tiled=True), "tensor", axis=0)
        all_dt = jnp.pad(all_dt.transpose(0, 2, 1), ((0, 0), (0, 16 - own_heads), (0, 0)))
        dt_weights = single(all_dt.reshape(parts * 16, width))
    rest = spread(jnp.concatenate([w_zx[:, 0], w_out]), order)
    z_weights = placed(rest, groups, (pl.ds(0, rows),), block_place)
    o_weights = placed(rest, groups, (pl.ds(rows, rows),), block_place)

    down_in = lax.dynamic_slice_in_dim(in_down, adapter, RANK, 1)
    down_out = lax.dynamic_slice_in_dim(out_down, adapter, RANK, 0)
    up_out = lax.dynamic_slice_in_dim(out_up, adapter, RANK, 0)
    gain = norm_gain.astype(f32)[None]
    convbc = jnp.pad(conv_bc.astype(f32), ((0, 3), (0, 0)))
    head_of = jnp.arange(inner) // (inner // heads)
    spread_heads = (jnp.arange(2 * heads)[:, None] % heads == head_of[None, :]).astype(bf16)
    head_sum = (head_of[:, None] == jnp.arange(heads)[None, :]).astype(bf16)

    (x, w_full, bc_full, dt_full, vec, up, normed, low, pre, values, scanned, keys, prebc, scal, states) = call_scan(
        info, gain, down_in, convbc, spread_heads,
        dict(x=x_pieces, w=x_weights, bc=bc_weights, dt=dt_weights, up=up_x, vec=vec_pieces),
        parts, heads, length, width, inner,
    )
    cot_pieces = paired(rows_of(cotangent), groups, parts, None, row_place)
    (mixed_rows, dlayer, dy, dot, back, low_back, up_z_grad, out_down_part, out_up_part) = call_gate(
        info, normed, low, scanned, x, vec, head_sum, down_out, up_out,
        dict(z=z_weights, o=o_weights, up=up_z, cot=cot_pieces),
    )

    def returned(array):
        return exchanged([lax.dynamic_slice_in_dim(array, (rank ^ k) * part_len, part_len, 0) for k in range(parts)])

    def stacked(blocks):
        result = jnp.zeros((parts,) + blocks[0].shape, blocks[0].dtype)
        for k, block in enumerate(blocks):
            result = lax.dynamic_update_index_in_dim(result, block, rank ^ k, 0)
        return result

    mixed = stacked([dealt(block, offsets[rank ^ k], group) for k, block in enumerate(returned(mixed_rows))])

    def at_adapter(part):
        return lax.dynamic_update_slice_in_dim(
            jnp.zeros((in_down.shape[1], part.shape[1]), bf16), part.astype(bf16), adapter, 0
        )

    early = lax.psum(at_adapter(jnp.concatenate([out_down_part, out_up_part], axis=1)), ("dp", "tensor"))
    early = early.astype(f32)

    token_rows, up_x_grad, in_down_part = call_back(
        (x, normed, low, dlayer, dy, values, pre, keys, prebc, scal, states, dot, back, low_back),
        (w_full, bc_full, dt_full, vec, up, gain, down_in, convbc, spread_heads, head_sum), parts, heads,
    )
    token_grad = stacked(returned(token_rows))
    in_up_part = at_adapter(jnp.concatenate([up_z_grad, up_x_grad], axis=1)).reshape(-1, 2, inner)
    in_up_grad = lax.psum_scatter(in_up_part, "tensor", scatter_dimension=2, tiled=True)
    in_up_grad = lax.psum(in_up_grad, "dp").astype(f32)
    in_down_grad = lax.psum(at_adapter(in_down_part), ("dp", "tensor")).astype(f32).T
    return (mixed, token_grad, in_down_grad, in_up_grad, early[:, :inner], early[:, inner:])


def solution(mesh):
    return jax.shard_map(
        on_device,
        mesh=mesh,
        in_specs=(
            P("dp", "tensor", None), P("dp", "tensor", None), P(), P(), P(), P(),
            P("dp", None, "tensor"), P("dp", None), P("dp", "tensor"), P("dp", "tensor"),
            P(None, "tensor"), P(), P("tensor"), P("tensor"), P("tensor"), P("tensor"),
            P(), P(None, None, "tensor"), P(), P(),
        ),
        out_specs=(
            P("dp", "tensor", None), P("dp", "tensor", None), P(), P(None, None, "tensor"), P(), P(),
        ),
        check_vma=False,
    )
```

time: 1960 us -> 827 us (0.42)
  matrix products: 465 us -> 0 us
  waiting for transfers between devices: 664 us -> 249 us
  other arithmetic: 266 us -> 18.6 us
  blocking collectives: 175 us -> 0 us
  Pallas kernels: 0 us -> 135 us
  starting transfers between devices: 11.1 us -> 80.4 us
  loops' own time: 23.5 us -> 0 us
  local copies, waits for them, and re-layouts: 328 us -> 308 us
    dot_general x76 -> x0, matrix products: 451 us -> none  [the longest x64 358 us: einsum_high(): return jnp.einsum(form, *operands, precision=lax.Precision.HIGHEST)]
    ppermute x6 -> x48, waiting for transfers between devices: 552 us -> 181 us  [moved(): return lax.ppermute(block, axis, [(i, route(i, size)) for i in range(size)])]
    unnamed x162 -> x112, local copies, waits for them, and re-layouts: 13.1 us -> 269 us
    all_gather x3 -> x0, blocking collectives: 165 us -> none  [the longest x1 107 us: on_device(): lax.all_gather(dt_columns, 'tensor', axis=2, tiled=True)]
    pallas_call x0 -> x3, Pallas kernels: none -> 135 us  [the longest x1 48.5 us: call_back(): pl.pallas_call(functools.partial(back_kernel, parts, heads), grid=(steps,...]
    another operation x49 -> x5, other arithmetic: 101 us -> 1.1 us
    ppermute x6 -> x48, starting transfers between devices: 4.86 us -> 80.1 us  [moved(): return lax.ppermute(block, axis, [(i, route(i, size)) for i in range(size)])]
    dynamic_slice x108 -> x10, local copies, waits for them, and re-layouts: 61.8 us -> 11.3 us  [the longest x2 3.67 us: returned(): lax.dynamic_slice_in_dim(array, (rank ^ k) * part_len, part_len, 0)]
  transfers between devices with their start and end apart: 18 -> 51, of which waited for: 8 -> 18; matrix products, arithmetic and copies ran while one was open for 24% -> 38% of each run, Pallas kernels for 0% -> 5%
where the time goes in v1:
time: 827 us; the launch traced here: 821 us
  local copies, waits for them, and re-layouts  308 us (37%)
  waiting for transfers between devices  249 us (30%)
  Pallas kernels  135 us (16%)
  starting transfers between devices  80.4 us (10%)
  between operations  29.3 us (4%)
  other arithmetic  18.6 us (2%)
    unnamed x112, local copies, waits for them, and re-layouts  269 us
    ppermute x48, waiting for transfers between devices, moved(): return lax.ppermute(block, axis, [(i, route(i, size)) for i in range(size)])  181 us
    ppermute x48, starting transfers between devices, moved(): return lax.ppermute(block, axis, [(i, route(i, size)) for i in range(size)])  80.1 us
    psum x1, waiting for transfers between devices, on_device(): in_up_grad = lax.psum(in_up_grad, 'dp').astype(f32)  68.5 us
    pallas_call x1, Pallas kernels, call_back(): pl.pallas_call(functools.partial(back_kernel, parts, heads), grid=(steps,...  48.5 us
    pallas_call x1, Pallas kernels, call_scan(): pl.pallas_call(functools.partial(scan_kernel, names, (owners, lists), cou...  44.1 us
    pallas_call x1, Pallas kernels, call_gate(): pl.pallas_call(functools.partial(gate_kernel, names, (owners, lists), cou...  42.9 us
  transfers between devices with their start and end apart: 51, of which 18 were waited for; matrix products, arithmetic and copies ran while one was open for 38% of the time, Pallas kernels for 5%

profile of v1, /device:TPU:0, one launch (start us, length us, event | category | flops | bytes accessed | tf_op | source)
XLA Modules:
  0.0 821.3 jit_solution(13206901100511046011)
XLA Ops:
  17.6 5.4 collective-permute-done.21
  23.0 10.4 %collective-permute-done.22 = bf16[1,256,512]{2,1,0:T(8,128)(2,1)S(1)} collective-permute-done((bf16[1,256,512]{2,1,0:T(8,128)(2,1)S(1)}, bf16[1,256,512]{2,1,0:T(8,128)(2,1)S(1)}, u32[]{:S(2)}, u32[]{:S(2)}) %collective-permute-start.22) | collective-permute-done | bytes 262176 | tf_op jit(solution)/shard_map/ppermute | solution.py:465
  38.4 20.2 %collective-permute-done.24 = bf16[4,256,512]{2,1,0:T(8,128)(2,1)S(1)} collective-permute-done((bf16[4,256,512]{2,1,0:T(8,128)(2,1)S(1)}, bf16[4,256,512]{2,1,0:T(8,128)(2,1)S(1)}, u32[]{:S(2)}, u32[]{:S(2)}) %collective-permute-start.24) | collective-permute-done | bytes 1048608 | tf_op jit(solution)/shard_map/ppermute | solution.py:465
  62.3 6.2 collective-permute-start.3
  71.5 35.3 %collective-permute-done.25 = bf16[8,256,512]{2,1,0:T(8,128)(2,1)S(1)} collective-permute-done((bf16[8,256,512]{2,1,0:T(8,128)(2,1)}, bf16[8,256,512]{2,1,0:T(8,128)(2,1)S(1)}, u32[]{:S(2)}, u32[]{:S(2)}) %collective-permute-start.25) | collective-permute-done | bytes 2097184 | tf_op jit(solution)/shard_map/ppermute | solution.py:465
  110.0 6.3 collective-permute-start.9
  136.6 12.2 %collective-permute-done.7 = bf16[8,128,512]{2,1,0:T(8,128)(2,1)} collective-permute-done((bf16[8,128,512]{2,1,0:T(8,128)(2,1)}, bf16[8,128,512]{2,1,0:T(8,128)(2,1)}, u32[]{:S(2)}, u32[]{:S(2)}) %collective-permute-start.7) | collective-permute-done | bytes 1048608 | tf_op jit(solution)/shard_map/ppermute | solution.py:465
  188.5 11.3 %collective-permute-done.1.refs_7_ = bf16[256,1024]{1,0:T(8,128)(2,1)S(1)} collective-permute-done((bf16[256,1024]{1,0:T(8,128)(2,1)}, bf16[256,1024]{1,0:T(8,128)(2,1)S(1)}, u32[]{:S(2)}, u32[]{:S(2)}) %collective-permute-start.1) | collective-permute-done | bytes 524320 | tf_op jit(solution)/shard_map/ppermute | solution.py:465
  199.8 10.8 %collective-permute-done.2.refs_8_ = bf16[256,1024]{1,0:T(8,128)(2,1)S(1)} collective-permute-done((bf16[256,1024]{1,0:T(8,128)(2,1)}, bf16[256,1024]{1,0:T(8,128)(2,1)S(1)}, u32[]{:S(2)}, u32[]{:S(2)}) %collective-permute-start.2) | collective-permute-done | bytes 524320 | tf_op jit(solution)/shard_map/ppermute | solution.py:465
  213.9 44.1 %shard_map.235 = (bf16[1024,1024]{1,0:T(8,128)(2,1)}, bf16[1024,2048]{1,0:T(8,128)(2,1)}, bf16[1024,256]{1,0:T(8,128)(2,1)}, bf16[32,1024]{1,0:T(8,128)(2,1)}, f...) custom-call(s32[17]{0:T(128)} %stack.76.refs_0_, ...), custom_call_target="tpu_custom_call" | custom-call | tf_op jit(solution)/shard_map/pallas_call | solution.py:220
  259.1 42.9 %shard_map.236 = (bf16[1024,1024]{1,0:T(8,128)(2,1)}, bf16[1024,1024]{1,0:T(8,128)(2,1)}, bf16[1024,2048]{1,0:T(8,128)(2,1)}, f32[1024,32]{1,0:T(8,128)}, f32[10...) custom-call(s32[17]{0:T(128)} %stack.76.refs_0_, ...), custom_call_target="tpu_custom_call" | custom-call | tf_op jit(solution)/shard_map/pallas_call | solution.py:316
  302.1 48.5 %shard_map.237 = (bf16[1024,1024]{1,0:T(8,128)(2,1)}, f32[16,2048]{1,0:T(8,128)}, f32[16,1024]{1,0:T(8,128)}) custom-call(bf16[1024,1024]{1,0:T(8,128)(2,1)} %get-tuple-element.48.refs_4_.refs_0_, bf16[1024,1024]{1,0:T(8,128)(2,1)} %get-tuple-element.45.refs_1_, bf16[1024,16]{1,0:T(8,128)(2,1)} %get-tuple-element.46.refs_2_, ...), custom_call_target="tpu_custom_call" | custom-call | tf_op jit(solution)/shard_map/pallas_call | solution.py:445
  367.8 102.6 %copy.40 = bf16[128,2,2048]{1,0,2:T(8,128)(2,1)} copy(bf16[128,2,2048]{2,1,0:T(2,128)(2,1)S(1)} %reshape.95) | data formatting | bytes 2097152
  470.5 97.2 %reshape.98 = bf16[2048,256]{1,0:T(8,128)(2,1)} reshape(bf16[2048,128,2]{2,1,0:T(8,128)(2,1)} %bitcast) | data formatting | bytes 2097152
  575.0 6.3 collective-permute-start.31
  588.4 6.5 collective-permute-start.43
  599.6 6.3 collective-permute-start.39
  605.9 3.8 collective-permute-done.34
  609.8 6.3 collective-permute-start.35
  619.3 10.2 %collective-permute-done.35 = bf16[256,1024]{1,0:T(8,128)(2,1)S(1)} collective-permute-done((bf16[256,1024]{1,0:T(8,128)(2,1)S(1)}, bf16[256,1024]{1,0:T(8,128)(2,1)S(1)}, u32[]{:S(2)}, u32[]{:S(2)}) %collective-permute-start.35) | collective-permute-done | bytes 524320 | tf_op jit(solution)/shard_map/ppermute | solution.py:465
  633.4 50.7 %collective-permute-done.32 = bf16[256,1024]{1,0:T(8,128)(2,1)S(1)} collective-permute-done((bf16[256,1024]{1,0:T(8,128)(2,1)S(1)}, bf16[256,1024]{1,0:T(8,128)(2,1)S(1)}, u32[]{:S(2)}, u32[]{:S(2)}) %collective-permute-start.32) | collective-permute-done | bytes 524320 | tf_op jit(solution)/shard_map/ppermute | solution.py:465
  684.6 37.9 %reshape.99 = bf16[512,128,2]{2,1,0:T(8,128)(2,1)} reshape(bf16[512,256]{1,0:T(8,128)(2,1)} %reduce-scatter.4.cloned.1.call-done) | data formatting | bytes 524288
  722.6 17.9 %copy.41 = bf16[128,2,512]{2,1,0:T(2,128)(2,1)} copy(bf16[128,2,512]{1,0,2:T(8,128)(2,1)} %bitcast.94) | data formatting | bytes 524288
  743.3 68.5 %all-reduce.6.cloned.1.call-done = bf16[128,2,512]{2,1,0:T(2,128)(2,1)} async-done(((bf16[128,2,512]{2,1,0:T(2,128)(2,1)}), bf16[128,2,512]{2,1,0:T(2,128)(2,1)}) %all-reduce.6.cloned.1.call-update) | async-done | bytes 262160 | tf_op jit(solution)/shard_map/psum | solution.py:661
  (273 shorter events, 124.2 us)
Async XLA Ops:
  8.0 559.7 %all-reduce.8.cloned.1.call-start = ((), (), s32[]{:S(2)}) async-start(), calls=%async_computation.3 | async-start | bytes 2097152 | tf_op jit(solution)/shard_map/psum | solution.py:662
  60.1 46.8 %collective-permute-start.25 = (bf16[8,256,512]{2,1,0:T(8,128)(2,1)}, bf16[8,256,512]{2,1,0:T(8,128)(2,1)S(1)}, u32[]{:S(2)}, u32[]{:S(2)}) collective-permute-start(bf16[8,256,512]{2,1,0:T(8,128)(2,1)} %get-tuple-element.91), channel_id=1, source_target_pairs={{0,2},{1,3},{2,0},{3,1},{4,6},{5,7},{6,4},{7,5},{8,10},{9,11},{10,... | collective-permute-start | bytes 6291464 | tf_op jit(solution)/shard_map/ppermute | solution.py:465
  62.3 46.1 %collective-permute-start.3 = (bf16[1,128,512]{2,1,0:T(8,128)(2,1)S(1)}, bf16[1,128,512]{2,1,0:T(8,128)(2,1)S(1)}, u32[]{:S(2)}, u32[]{:S(2)}) collective-permute-start(bf16[1,128,512]{2,1,0:T(8,128)(2,1)S(1)} %get-tuple-element.75), channel_id=1, source_target_pairs={{0,8},{4,12},{8,16},{12,20},{16,24},{20,28},{24,0},{28,4},{1,9},{5... | collective-permute-start | bytes 393224 | tf_op jit(solution)/shard_map/ppermute | solution.py:465
  68.4 39.9 %collective-permute-start.4 = (bf16[1,128,512]{2,1,0:T(8,128)(2,1)S(1)}, bf16[1,128,512]{2,1,0:T(8,128)(2,1)S(1)}, u32[]{:S(2)}, u32[]{:S(2)}) collective-permute-start(bf16[1,128,512]{2,1,0:T(8,128)(2,1)S(1)} %get-tuple-element.75), channel_id=1, source_target_pairs={{0,16},{4,20},{8,24},{12,28},{16,0},{20,4},{24,8},{28,12},{1,17},{... | collective-permute-start | bytes 393224 | tf_op jit(solution)/shard_map/ppermute | solution.py:465
  69.0 39.4 %collective-permute-start.5 = (bf16[1,128,512]{2,1,0:T(8,128)(2,1)S(1)}, bf16[1,128,512]{2,1,0:T(8,128)(2,1)S(1)}, u32[]{:S(2)}, u32[]{:S(2)}) collective-permute-start(bf16[1,128,512]{2,1,0:T(8,128)(2,1)S(1)} %get-tuple-element.75), channel_id=1, source_target_pairs={{0,24},{4,28},{8,0},{12,4},{16,8},{20,12},{24,16},{28,20},{1,25},{... | collective-permute-start | bytes 393224 | tf_op jit(solution)/shard_map/ppermute | solution.py:465
  108.4 149.7 %collective-permute-start.26 = (bf16[16,256,512]{2,1,0:T(8,128)(2,1)}, bf16[16,256,512]{2,1,0:T(8,128)(2,1)}, u32[]{:S(2)}, u32[]{:S(2)}) collective-permute-start(bf16[16,256,512]{2,1,0:T(8,128)(2,1)} %constant_dynamic-update-slice_fusion.27.refs_9_.refs_11_), channel_id=1, source_target_pairs={{0,1},{1,0},{2,3},{3,2},{4,5},{5,4},{6,7},{7,6},{8,9},{9,8},{10,11... | collective-permute-start | bytes 12582920 | tf_op jit(solution)/shard_map/ppermute | solution.py:465
  110.0 42.5 %collective-permute-start.9 = (bf16[1,48,256]{2,1,0:T(8,128)(2,1)S(1)}, bf16[1,48,256]{2,1,0:T(8,128)(2,1)S(1)}, u32[]{:S(2)}, u32[]{:S(2)}) collective-permute-start(bf16[1,48,256]{2,1,0:T(8,128)(2,1)S(1)} %fusion.3), channel_id=1, source_target_pairs={{0,8},{4,12},{8,16},{12,20},{16,24},{20,28},{24,0},{28,4},{1,9},{5... | collective-permute-start | bytes 73736 | tf_op jit(solution)/shard_map/ppermute | solution.py:465
  116.4 39.0 %collective-permute-start.11 = (bf16[1,48,256]{2,1,0:T(8,128)(2,1)S(1)}, bf16[1,48,256]{2,1,0:T(8,128)(2,1)S(1)}, u32[]{:S(2)}, u32[]{:S(2)}) collective-permute-start(bf16[1,48,256]{2,1,0:T(8,128)(2,1)S(1)} %fusion.3), channel_id=1, source_target_pairs={{0,24},{4,28},{8,0},{12,4},{16,8},{20,12},{24,16},{28,20},{1,25},{... | collective-permute-start | bytes 73736 | tf_op jit(solution)/shard_map/ppermute | solution.py:465
  150.1 63.7 %collective-permute-start.8 = (bf16[16,128,512]{2,1,0:T(8,128)(2,1)S(1)}, bf16[16,128,512]{2,1,0:T(8,128)(2,1)}, u32[]{:S(2)}, u32[]{:S(2)}) collective-permute-start(bf16[16,128,512]{2,1,0:T(8,128)(2,1)S(1)} %constant_dynamic-update-slice_fusion.5.refs_9_), channel_id=1, source_target_pairs={{0,1},{1,0},{2,3},{3,2},{4,5},{5,4},{6,7},{7,6},{8,9},{9,8},{10,11... | collective-permute-start | bytes 6291464 | tf_op jit(solution)/shard_map/ppermute | solution.py:465
  199.8 58.2 %collective-permute-start.27 = (bf16[256,1024]{1,0:T(8,128)(2,1)}, bf16[256,1024]{1,0:T(8,128)(2,1)S(1)}, u32[]{:S(2)}, u32[]{:S(2)}) collective-permute-start(bf16[256,1024]{1,0:T(8,128)(2,1)} %get-tuple-element.84), channel_id=1, source_target_pairs={{0,1},{1,0},{2,3},{3,2},{4,5},{5,4},{6,7},{7,6},{8,9},{9,8},{10,11... | collective-permute-start | bytes 1572872 | tf_op jit(solution)/shard_map/ppermute | solution.py:465
  210.6 47.4 %collective-permute-start.28 = (bf16[256,1024]{1,0:T(8,128)(2,1)}, bf16[256,1024]{1,0:T(8,128)(2,1)S(1)}, u32[]{:S(2)}, u32[]{:S(2)}) collective-permute-start(bf16[256,1024]{1,0:T(8,128)(2,1)} %get-tuple-element.86), channel_id=1, source_target_pairs={{0,2},{1,3},{2,0},{3,1},{4,6},{5,7},{6,4},{7,5},{8,10},{9,11},{10,... | collective-permute-start | bytes 1572872 | tf_op jit(solution)/shard_map/ppermute | solution.py:465
  211.7 46.3 %collective-permute-start.29 = (bf16[256,1024]{1,0:T(8,128)(2,1)}, bf16[256,1024]{1,0:T(8,128)(2,1)S(1)}, u32[]{:S(2)}, u32[]{:S(2)}) collective-permute-start(bf16[256,1024]{1,0:T(8,128)(2,1)} %get-tuple-element.83), channel_id=1, source_target_pairs={{0,3},{1,2},{2,1},{3,0},{4,7},{5,6},{6,5},{7,4},{8,11},{9,10},{10,... | collective-permute-start | bytes 1572872 | tf_op jit(solution)/shard_map/ppermute | solution.py:465
  354.9 220.2 %collective-permute-start.46 = (bf16[256,1024]{1,0:T(8,128)(2,1)}, bf16[256,1024]{1,0:T(8,128)(2,1)}, u32[]{:S(2)}, u32[]{:S(2)}) collective-permute-start(bf16[256,1024]{1,0:T(8,128)(2,1)} %get-tuple-element.77), channel_id=1, source_target_pairs={{0,2},{1,3},{2,0},{3,1},{4,6},{5,7},{6,4},{7,5},{8,10},{9,11},{10,... | collective-permute-start | bytes 1572872 | tf_op jit(solution)/shard_map/ppermute | solution.py:465
  357.2 215.1 %collective-permute-start.41 = (bf16[256,1024]{1,0:T(8,128)(2,1)}, bf16[256,1024]{1,0:T(8,128)(2,1)}, u32[]{:S(2)}, u32[]{:S(2)}) collective-permute-start(bf16[256,1024]{1,0:T(8,128)(2,1)} %get-tuple-element.79), channel_id=1, source_target_pairs={{0,3},{1,2},{2,1},{3,0},{4,7},{5,6},{6,5},{7,4},{8,11},{9,10},{10,... | collective-permute-start | bytes 1572872 | tf_op jit(solution)/shard_map/ppermute | solution.py:465
  357.4 223.9 %collective-permute-start.37 = (bf16[256,1024]{1,0:T(8,128)(2,1)}, bf16[256,1024]{1,0:T(8,128)(2,1)}, u32[]{:S(2)}, u32[]{:S(2)}) collective-permute-start(bf16[256,1024]{1,0:T(8,128)(2,1)} %get-tuple-element.80), channel_id=1, source_target_pairs={{0,2},{1,3},{2,0},{3,1},{4,6},{5,7},{6,4},{7,5},{8,10},{9,11},{10,... | collective-permute-start | bytes 1572872 | tf_op jit(solution)/shard_map/ppermute | solution.py:465
  358.6 213.1 %collective-permute-start.30 = (bf16[256,1024]{1,0:T(8,128)(2,1)S(1)}, bf16[256,1024]{1,0:T(8,128)(2,1)}, u32[]{:S(2)}, u32[]{:S(2)}) collective-permute-start(bf16[256,1024]{1,0:T(8,128)(2,1)S(1)} %get-tuple-element.82), channel_id=1, source_target_pairs={{0,4},{4,0},{8,12},{12,8},{16,20},{20,16},{24,28},{28,24},{1,5},{5... | collective-permute-start | bytes 1572872 | tf_op jit(solution)/shard_map/ppermute | solution.py:465
  362.9 321.7 %reduce-scatter.4.cloned.1.call-start = ((), (), s32[]{:S(2)}) async-start(), calls=%async_computation.2 | async-start | bytes 1310720
  363.3 219.3 %collective-permute-start.33 = (bf16[256,1024]{1,0:T(8,128)(2,1)}, bf16[256,1024]{1,0:T(8,128)(2,1)}, u32[]{:S(2)}, u32[]{:S(2)}) collective-permute-start(bf16[256,1024]{1,0:T(8,128)(2,1)} %get-tuple-element.81), channel_id=1, source_target_pairs={{0,1},{1,0},{2,3},{3,2},{4,5},{5,4},{6,7},{7,6},{8,9},{9,8},{10,11... | collective-permute-start | bytes 1572872 | tf_op jit(solution)/shard_map/ppermute | solution.py:465
  567.7 244.1 %all-reduce.6.cloned.1.call-start = ((), (), s32[]{:S(2)}) async-start(), calls=%async_computation.1 | async-start | bytes 524288 | tf_op jit(solution)/shard_map/psum | solution.py:661
  575.0 41.1 %collective-permute-start.31 = (bf16[256,1024]{1,0:T(8,128)(2,1)S(1)}, bf16[256,1024]{1,0:T(8,128)(2,1)S(1)}, u32[]{:S(2)}, u32[]{:S(2)}) collective-permute-start(bf16[256,1024]{1,0:T(8,128)(2,1)S(1)} %broadcast_select_fusion.6), channel_id=1, source_target_pairs={{0,8},{4,12},{8,16},{12,20},{16,24},{20,28},{24,0},{28,4},{1,9},{5... | collective-permute-start | bytes 1572872 | tf_op jit(solution)/shard_map/ppermute | solution.py:465
  616.2 68.0 %collective-permute-start.32 = (bf16[256,1024]{1,0:T(8,128)(2,1)S(1)}, bf16[256,1024]{1,0:T(8,128)(2,1)S(1)}, u32[]{:S(2)}, u32[]{:S(2)}) collective-permute-start(bf16[256,1024]{1,0:T(8,128)(2,1)S(1)} %broadcast_select_fusion.7), channel_id=1, source_target_pairs={{0,16},{4,20},{8,24},{12,28},{16,0},{20,4},{24,8},{28,12},{1,17},{... | collective-permute-start | bytes 1572872 | tf_op jit(solution)/shard_map/ppermute | solution.py:465
  616.3 126.8 %collective-permute-start.44 = (bf16[256,1024]{1,0:T(8,128)(2,1)S(1)}, bf16[256,1024]{1,0:T(8,128)(2,1)}, u32[]{:S(2)}, u32[]{:S(2)}) collective-permute-start(bf16[256,1024]{1,0:T(8,128)(2,1)S(1)} %broadcast_select_fusion.1), channel_id=1, source_target_pairs={{0,16},{4,20},{8,24},{12,28},{16,0},{20,4},{24,8},{28,12},{1,17},{... | collective-permute-start | bytes 1572872 | tf_op jit(solution)/shard_map/ppermute | solution.py:465
  629.6 110.9 %collective-permute-start.36 = (bf16[256,1024]{1,0:T(8,128)(2,1)S(1)}, bf16[256,1024]{1,0:T(8,128)(2,1)}, u32[]{:S(2)}, u32[]{:S(2)}) collective-permute-start(bf16[256,1024]{1,0:T(8,128)(2,1)S(1)} %broadcast_select_fusion.5), channel_id=1, source_target_pairs={{0,16},{4,20},{8,24},{12,28},{16,0},{20,4},{24,8},{28,12},{1,17},{... | collective-permute-start | bytes 1572872 | tf_op jit(solution)/shard_map/ppermute | solution.py:465
  632.4 109.4 %collective-permute-start.40 = (bf16[256,1024]{1,0:T(8,128)(2,1)}, bf16[256,1024]{1,0:T(8,128)(2,1)}, u32[]{:S(2)}, u32[]{:S(2)}) collective-permute-start(bf16[256,1024]{1,0:T(8,128)(2,1)} %broadcast_select_fusion.3), channel_id=1, source_target_pairs={{0,16},{4,20},{8,24},{12,28},{16,0},{20,4},{24,8},{28,12},{1,17},{... | collective-permute-start | bytes 1572872 | tf_op jit(solution)/shard_map/ppermute | solution.py:465
  (73 other events, 1650.5 us)
Sparse Core Ops, SparseCore 0:
  363.1 132.4 all-reduce.7
Sparse Core Ops, SparseCore 1:
  567.8 27.1 reduce-scatter.3
  740.6 71.2 all-reduce.5
